TPU v7x, 128 devices: a whole 4x4x4 slice. The times are simulated.
128 devices in a mesh: pp: 8 (over x_hi, y), tp: 16 (over x_lo, z, core).
Axes of the slice: x: 4 (x_hi: 2, x_lo: 2; x = x_hi * 2 + x_lo), y: 4, z: 4, core: 2. Of those that a mesh axis runs over, the one named last changes fastest.
Arguments:
- input_codes: bfloat16 [8, 256, 8192], P('pp', 'tp'), may hold values from -127 to 127
- input_exps: int32 [8, 64], P('pp'), may hold values from -7 to -4
- prefix_len: int32 [8], P('pp'), may hold values from 2048 to 8192, as said below
- norm_gain: bfloat16 [8, 8192], P('pp'), may hold values from 0.099609375 to 1.8984375
- w_query: bfloat16 [8, 8192, 8192], P('pp', None, 'tp'), may hold values from -0.0625 to 0.0625
- w_keyval: bfloat16 [8, 8192, 16, 256], P('pp', None, 'tp'), as said below
- w_out: bfloat16 [8, 8192, 8192], P('pp', 'tp'), may hold values from -1.5 to 1.5
- kv_cache: bfloat16 [8, 16, 8192, 256], P('pp', 'tp'), as said below
- partial_exps: int32 [8, 64], P('pp'), may hold values from -10 to -7
- share_exps: int32 [8, 64], P('pp'), may hold values from -2 to 0
- output_exps: int32 [8, 64], replicated, may hold values from -7 to -4
Outputs:
- received: bfloat16 [8, 256, 8192], P('pp', 'tp')
Inputs may be any that keep to these rules, and one draw needn't show every extreme that they name: `prefix_len`: each section's length lies in 2048 to 8192, and some section has exactly 8192. `w_keyval`: along the third dimension, the 2 entries 2 * g to 2 * g + 1 are equal (one key and value head for them). `kv_cache`: along the second dimension, the 2 entries 2 * g to 2 * g + 1 are equal (one key and value head for them).
All inputs are finite; a program needn't handle non-finite values.
Results may differ from a plain program's by a relative error of at most 0.029.
The roundings to bfloat16 on the way count: a program that leaves them out, or rounds other values in their place, can miss the bound.
Values may be sent and summed in bfloat16 or wider, within the bound.
A program may use at most 128 MiB of HBM per device.

v0:
```python
import math

import jax
import jax.numpy as jnp
from jax import lax
from jax.sharding import PartitionSpec as P

EPSILON = 1e-05
ROPE_BASE = 500000.0


def shifted(value, axis, steps):
    count = lax.axis_size(axis)
    pairs = [(source, (source + steps) % count) for source in range(count)]
    return lax.ppermute(value, axis, pairs)


def group_scale(exponents, group_size):
    return jnp.repeat(jnp.exp2(exponents.astype(jnp.float32)), group_size)


def rope_tables(positions, head_dim):
    half_dim = head_dim // 2
    freqs = jnp.power(
        jnp.float32(ROPE_BASE), -2.0 * jnp.arange(half_dim, dtype=jnp.float32) / head_dim
    )
    angles = positions.astype(jnp.float32)[:, None] * freqs[None, :]
    return (jnp.cos(angles), jnp.sin(angles))


def apply_rotary(values, cosine, sine):
    half_dim = values.shape[-1] // 2
    first_half = values[..., :half_dim]
    second_half = values[..., half_dim:]
    return jnp.concatenate(
        [first_half * cosine - second_half * sine, second_half * cosine + first_half * sine],
        axis=-1,
    )


def attention(queries, new_keys, new_values, cache_keys, cache_values, length):
    total_rows, head_count, head_dim = queries.shape
    block_rows = min(total_rows, 256)
    scale = 1.0 / math.sqrt(head_dim)
    cache_live = jnp.arange(cache_keys.shape[0], dtype=jnp.int32) < length
    key_index = jnp.arange(total_rows, dtype=jnp.int32)
    blocks = queries.reshape(total_rows // block_rows, block_rows, head_count, head_dim)
    starts = jnp.arange(total_rows // block_rows, dtype=jnp.int32) * block_rows

    def one_block(pair):
        query_block, start = pair
        old_scores = (
            jnp.einsum("qhd,kd->hqk", query_block, cache_keys, preferred_element_type=jnp.float32)
            * scale
        )
        old_scores = jnp.where(cache_live[None, None, :], old_scores, -jnp.inf)
        query_index = start + jnp.arange(block_rows, dtype=jnp.int32)
        new_scores = (
            jnp.einsum("qhd,kd->hqk", query_block, new_keys, preferred_element_type=jnp.float32)
            * scale
        )
        new_scores = jnp.where(
            key_index[None, None, :] <= query_index[None, :, None], new_scores, -jnp.inf
        )
        highest = jnp.maximum(
            jnp.max(old_scores, axis=-1, keepdims=True), jnp.max(new_scores, axis=-1, keepdims=True)
        )
        old_weights = jnp.exp(old_scores - highest)
        new_weights = jnp.exp(new_scores - highest)
        denominator = jnp.sum(old_weights, axis=-1, keepdims=True) + jnp.sum(
            new_weights, axis=-1, keepdims=True
        )
        old_weights = (old_weights / denominator).astype(jnp.bfloat16)
        new_weights = (new_weights / denominator).astype(jnp.bfloat16)
        mixed = jnp.einsum(
            "hqk,kd->qhd", old_weights, cache_values, preferred_element_type=jnp.float32
        )
        mixed = mixed + jnp.einsum(
            "hqk,kd->qhd", new_weights, new_values, preferred_element_type=jnp.float32
        )
        return mixed.astype(jnp.bfloat16)

    mixed = lax.map(one_block, (blocks, starts))
    return mixed.reshape(total_rows, head_count * head_dim)


def local(
    input_codes,
    input_exps,
    prefix_len,
    norm_gain,
    w_query,
    w_keyval,
    w_out,
    kv_cache,
    partial_exps,
    share_exps,
    output_exps,
):
    tp_count = lax.axis_size("tp")
    my_rank = lax.axis_index("tp")
    section_rank = lax.axis_index("pp")
    section_count = lax.axis_size("pp")
    model_width = input_codes.shape[2]
    own_rows = input_codes.shape[1]
    group_size = model_width // input_exps.shape[1]
    head_dim = w_keyval.shape[3] // 2
    local_heads = w_query.shape[2] // head_dim
    query_cols = local_heads * head_dim
    scale_in = group_scale(input_exps[0], group_size)
    gain_row = norm_gain[0].astype(jnp.float32)
    query_weight = w_query[0]
    keyval_weight = w_keyval[0, :, 0, :]
    resid_rows = (
        lax.all_gather(input_codes[0], "tp", axis=0, tiled=True).astype(jnp.float32) * scale_in
    )
    power = jnp.mean(resid_rows * resid_rows, axis=-1, keepdims=True)
    normed = (resid_rows * lax.rsqrt(power + EPSILON) * gain_row).astype(jnp.bfloat16)
    projected = jnp.concatenate(
        [
            jnp.dot(normed, query_weight, preferred_element_type=jnp.float32),
            jnp.dot(normed, keyval_weight, preferred_element_type=jnp.float32),
        ],
        axis=1,
    )
    total_rows = projected.shape[0]
    length = prefix_len[0]
    positions = length + jnp.arange(total_rows, dtype=jnp.int32)
    cosine, sine = rope_tables(positions, head_dim)
    rot_query = apply_rotary(
        projected[:, :query_cols].reshape(total_rows, local_heads, head_dim),
        cosine[:, None, :],
        sine[:, None, :],
    ).astype(jnp.bfloat16)
    new_keys = apply_rotary(projected[:, query_cols : query_cols + head_dim], cosine, sine).astype(
        jnp.bfloat16
    )
    new_values = projected[:, query_cols + head_dim :].astype(jnp.bfloat16)
    cache = kv_cache[0, 0]
    attended = attention(
        rot_query, new_keys, new_values, cache[:, :head_dim], cache[:, head_dim:], length
    )
    part_scale = group_scale(partial_exps[0], group_size)
    inverse_part = group_scale(-partial_exps[0], group_size)
    share_scale = group_scale(share_exps[0], group_size)
    inverse_share = group_scale(-share_exps[0], group_size)
    out_weight = w_out[0]
    slice_width = model_width // tp_count
    slice_start = my_rank * slice_width
    partial_value = jnp.dot(attended, out_weight, preferred_element_type=jnp.float32)
    codes8 = jnp.clip(partial_value * inverse_part, -127.0, 127.0).astype(jnp.bfloat16)
    codes8 = lax.optimization_barrier(codes8).astype(jnp.float32)
    own_part = lax.dynamic_slice_in_dim(part_scale, slice_start, slice_width, 0)
    own_inverse = lax.dynamic_slice_in_dim(inverse_share, slice_start, slice_width, 0)
    total = lax.psum_scatter(
        codes8.astype(jnp.bfloat16), "tp", scatter_dimension=1, tiled=True
    ).astype(jnp.float32)
    codes4 = jnp.clip(total * own_part * own_inverse, -7.0, 7.0).astype(jnp.bfloat16)
    codes4 = lax.optimization_barrier(codes4)
    whole_shares = lax.all_gather(codes4, "tp", axis=1, tiled=True)
    share_rows = lax.dynamic_slice_in_dim(whole_shares, my_rank * own_rows, own_rows, 0)
    resid_own = input_codes[0].astype(jnp.float32) * scale_in
    updated = resid_own + share_rows.astype(jnp.float32) * share_scale
    own_exps = lax.dynamic_index_in_dim(output_exps, section_rank, 0, keepdims=False)
    out_codes = jnp.clip(updated * group_scale(-own_exps, group_size), -127.0, 127.0).astype(
        jnp.bfloat16
    )
    out_codes = lax.optimization_barrier(out_codes)
    arrived = shifted(out_codes, "pp", 1)
    sender = (section_rank + section_count - 1) % section_count
    sender_exps = lax.dynamic_index_in_dim(output_exps, sender, 0, keepdims=False)
    decoded = (arrived.astype(jnp.float32) * group_scale(sender_exps, group_size)).astype(
        jnp.bfloat16
    )
    return decoded[None]


def solution(mesh):
    in_specs = (
        P("pp", "tp", None),
        P("pp", None),
        P("pp"),
        P("pp", None),
        P("pp", None, "tp"),
        P("pp", None, "tp", None),
        P("pp", "tp", None),
        P("pp", "tp", None, None),
        P("pp", None),
        P("pp", None),
        P(),
    )
    out_specs = P("pp", "tp", None)
    return jax.shard_map(local, mesh=mesh, in_specs=in_specs, out_specs=out_specs, check_vma=False)
```

profile of v0, /device:TPU:1, one launch (start us, length us, event | category | flops | bytes accessed | tf_op | source)
XLA Modules:
  0.0 239.3 jit_solution(151347399745264101)
XLA Ops:
  6.5 0.0 all-gather.6.cloned.1.call-start
  6.5 0.7 all-gather.6.cloned.1.call-update
  7.3 0.0 reduce-scatter.2.cloned.1.call-start
  7.3 0.8 mul.225
  8.7 0.0 copy-start.3
  8.8 0.0 copy-start.4
  8.8 12.0 %copy.23 = bf16[512,8192]{1,0:T(8,128)(2,1)} copy(bf16[512,8192]{0,1:T(8,128)(2,1)} %bitcast.104) | data formatting | bytes 16777216 | tf_op jit(solution)/shard_map/dot_general | solution.py:121
  20.8 0.0 copy-done.3
  20.9 0.0 copy-done.4
  20.9 0.1 broadcast_bitcast_fusion.6
  20.9 0.1 broadcast_bitcast_fusion.5
  21.0 29.1 %all-gather.6.cloned.1.call-done = bf16[1,256,8192]{2,1,0:T(8,128)(2,1)} async-done(((bf16[1,16,8192]{2,1,0:T(8,128)(2,1)}), bf16[1,256,8192]{2,1,0:T(8,128)(2,1)}) %all-gather.6.cloned.1.call-update) | async-done | bytes 4194320 | tf_op jit(solution)/shard_map/all_gather | solution.py:115
  50.1 3.5 %fusion.7 = f32[256]{0:T(256)S(1)} fusion(bf16[1,256,8192]{2,1,0:T(8,128)(2,1)} %all-gather.6.cloned.1.call-done, f32[8192]{0:T(1024)S(1)} %broadcast_bitcast_fusion.6), kind=kLoop, calls=%fused_computation.13 | loop fusion | flops 8388352 | bytes 4228096 | tf_op jit(solution)/shard_map/reduce_sum | solution.py:117
  53.7 5.9 %fusion.11 = f32[256,256]{0,1:T(8,128)S(1)} fusion(bf16[1,8192,1,256]{3,1,2,0:T(8,128)(2,1)} %param.16, bf16[1,256,8192]{2,1,0:T(8,128)(2,1)} %all-gather.6.cloned.1.call-done, f32[8192]{0:T(1024)S(1)} %bitcast.110, f32[256]{0:T(256)S(1)} %add_rsqrt_fusion, f32[8192]{0:T(1024)S(1)} %broadcast_bitcast_fusion.6), kind=kOutput, calls=%fused_computation.17 | convolution fusion | flops 1084227584 | bytes 8717312 | tf_op jit(solution)/shard_map/dot_general | solution.py:122
  59.5 0.3 subtract_convert_fusion.1
  59.9 0.0 slice-done
  59.9 0.0 copy-done
  59.9 0.0 copy-start.2
  59.9 2.6 %fusion.13 = f32[256,4,128]{0,2,1:T(8,128)S(1)} fusion(bf16[4,128,8192]{2,1,0:T(8,128)(2,1)S(1)} %bitcast.107, bf16[1,256,8192]{2,1,0:T(8,128)(2,1)S(1)} %copy-done, f32[8192]{0:T(1024)S(1)} %bitcast.111, f32[256]{0:T(256)S(1)} %add_rsqrt_fusion, f32[8192]{0:T(1024)S(1)} %broadcast_bitcast_fusion.6), kind=kOutput, calls=%fused_computation.19 | convolution fusion | flops 2157969408 | bytes 13173760 | tf_op jit(solution)/shard_map/dot_general | solution.py:121
  62.5 0.1 subtract_convert_fusion
  62.6 13.3 %bitcast_reduce_fusion = (f32[4,256]{1,0:T(4,128)S(1)}, f32[256,4,8192]{2,0,1:T(8,128)}) fusion(pred[8192]{0:T(1024)(128)(4,1)S(1)} %iota_compare_fusion.1, bf16[8192,256]{1,0:T(8,128)(2,1)S(1)} %bitcast.109, bf16[256,4,64]{0,2,1:T(8,128)(2,1)S(1)} %get-tuple-element.22, bf16[256,4,64]{0,2,1:T(8,128)(2,1)S(1)} %get-tuple-element.21), kind=kOutput, calls=%fused_computation.1 | convolution fusion | flops 2173172736 | bytes 35926016 | tf_op jit(solution)/shard_map/while/body/eval_jaxpr/qhd,kd->hqk/dot_general | solution.py:53
  75.9 0.3 fusion.44
  76.3 0.2 fusion.21
  76.5 15.0 %fusion.1 = f32[4,256]{1,0:T(4,128)S(1)} fusion(f32[256,4,8192]{2,0,1:T(8,128)} %get-tuple-element.45, f32[4,256]{1,0:T(4,128)S(1)} %max.30, pred[8192]{0:T(1024)(128)(4,1)S(1)} %iota_compare_fusion.1), kind=kLoop, calls=%fused_computation.5 | loop fusion | flops 33553408 | bytes 33570816 | tf_op jit(solution)/shard_map/while/body/eval_jaxpr/reduce_sum | solution.py:70
  91.5 14.9 %fusion.19 = f32[256,4,128]{0,2,1:T(8,128)S(1)} fusion(bf16[8192,256]{1,0:T(8,128)(2,1)} %bitcast.108, f32[256,4,8192]{2,0,1:T(8,128)} %get-tuple-element.45, f32[4,256]{1,0:T(4,128)S(1)} %add.80, f32[4,256]{1,0:T(4,128)S(1)} %max.30, pred[8192]{0:T(1024)(128)(4,1)S(1)} %iota_compare_fusion.1), kind=kOutput, calls=%fused_computation.29 | convolution fusion | flops 2189426688 | bytes 36192256 | tf_op jit(solution)/shard_map/while/body/eval_jaxpr/hqk,kd->qhd/dot_general | solution.py:75
  106.4 0.3 fusion.20
  106.7 0.0 copy-start.5
  106.7 0.0 copy-start.1
  106.7 7.9 %fusion.4 = bf16[256,8192]{1,0:T(8,128)(2,1)} fusion(bf16[256,512]{0,1:T(8,128)(2,1)S(1)} %bitcast.112, bf16[1,512,8192]{2,1,0:T(8,128)(2,1)} %param.17, f32[8192]{0:T(1024)S(1)} %broadcast_bitcast_fusion.5), kind=kOutput, calls=%fused_computation.9 | convolution fusion | flops 2153775104 | bytes 12877824 | tf_op jit(solution)/shard_map/dot_general | solution.py:150
  114.7 0.0 reduce-scatter.2.cloned.1.call-update
  114.7 0.0 all-gather.4.cloned.1.call-start
  114.8 0.1 broadcast_bitcast_fusion.4
  114.8 0.1 dynamic_slice.22
  114.9 0.0 copy-done.5
  114.9 0.1 broadcast_bitcast_fusion.3
  115.0 0.1 dynamic_slice.23
  115.1 62.4 %reduce-scatter.2.cloned.1.call-done = bf16[256,512]{1,0:T(8,128)(2,1)} async-done(((bf16[256,8192]{1,0:T(8,128)(2,1)}), bf16[256,512]{1,0:T(8,128)(2,1)}) %reduce-scatter.2.cloned.1.call-update) | async-done | bytes 262160 | tf_op jit(solution)/shard_map/reduce_scatter | solution.py:155
  177.5 1.7 clamp_convert_fusion
  179.2 0.0 all-gather.4.cloned.1.call-update
  179.3 0.8 fusion.39
  180.1 0.1 broadcast_bitcast_fusion.1
  180.1 39.5 %all-gather.4.cloned.1.call-done = bf16[256,8192]{1,0:T(8,128)(2,1)} async-done(((bf16[256,512]{1,0:T(8,128)(2,1)}), bf16[256,8192]{1,0:T(8,128)(2,1)}) %all-gather.4.cloned.1.call-update) | async-done | bytes 4194320 | tf_op jit(solution)/shard_map/all_gather | solution.py:160
  219.7 0.0 copy-done.1
  219.7 1.1 fusion.27
  220.8 1.3 collective-permute-start
  222.0 0.1 broadcast_bitcast_fusion
  222.1 10.0 %collective-permute-done = bf16[16,8192]{1,0:T(8,128)(2,1)S(1)} collective-permute-done((bf16[16,8192]{1,0:T(8,128)(2,1)S(1)}, bf16[16,8192]{1,0:T(8,128)(2,1)S(1)}, u32[]{:S(2)}, u32[]{:S(2)}) %collective-permute-start) | collective-permute-done | bytes 262176 | tf_op jit(solution)/shard_map/ppermute | solution.py:15
  232.1 0.8 fusion.28
  (16 shorter events, 0.1 us)
Async XLA Ops:
  6.5 43.6 %all-gather.6.cloned.1.call-start = ((), (), s32[]{:S(2)}) async-start(), calls=%async_computation.3 | async-start | bytes 4456448 | tf_op jit(solution)/shard_map/all_gather | solution.py:115
  7.3 170.3 %reduce-scatter.2.cloned.1.call-start = ((), (), s32[]{:S(2)}) async-start(), calls=%async_computation.1 | async-start | bytes 4456448 | tf_op jit(solution)/shard_map/reduce_scatter | solution.py:155
  8.7 12.1 %copy-start.3 = (s32[1,64]{1,0:T(1,128)S(1)}, s32[1,64]{1,0:T(1,128)}, u32[]{:S(2)}) copy-start(s32[1,64]{1,0:T(1,128)} %param.12) | copy-start | bytes 772
  8.8 12.1 %copy-start.4 = (s32[1,64]{1,0:T(1,128)S(1)}, s32[1,64]{1,0:T(1,128)}, u32[]{:S(2)}) copy-start(s32[1,64]{1,0:T(1,128)} %param.19) | copy-start | bytes 772
  50.1 9.7 %slice-start = ((s8[8388608]{0:T(1024)(128)(4,1)}), s8[4194304]{0:T(1024)(128)(4,1)S(1)}, s32[]{:S(2)}) async-start(s8[8388608]{0:T(1024)(128)(4,1)} %bitcast.105), calls=%async_computation.4 | async-start | bytes 8388608
  50.1 9.7 %copy-start = (bf16[1,256,8192]{2,1,0:T(8,128)(2,1)S(1)}, bf16[1,256,8192]{2,1,0:T(8,128)(2,1)}, u32[]{:S(2)}) copy-start(bf16[1,256,8192]{2,1,0:T(8,128)(2,1)} %all-gather.6.cloned.1.call-done) | copy-start | bytes 12582916
  53.7 6.2 %slice-start.1 = ((s8[8388608]{0:T(1024)(128)(4,1)}), s8[4194304]{0:T(1024)(128)(4,1)S(1)}, s32[]{:S(2)}) async-start(s8[8388608]{0:T(1024)(128)(4,1)} %bitcast.105), calls=%async_computation.5 | async-start | bytes 8388608
  59.9 2.7 %copy-start.2 = (bf16[1,1,8192,256]{3,2,1,0:T(8,128)(2,1)S(1)}, bf16[1,1,8192,256]{3,2,1,0:T(8,128)(2,1)}, u32[]{:S(2)}) copy-start(bf16[1,1,8192,256]{3,2,1,0:T(8,128)(2,1)} %param.18) | copy-start | bytes 12582916
  106.7 8.2 %copy-start.5 = (s32[1,64]{1,0:T(1,128)S(1)}, s32[1,64]{1,0:T(1,128)}, u32[]{:S(2)}) copy-start(s32[1,64]{1,0:T(1,128)} %param.20) | copy-start | bytes 772
  106.7 112.9 %copy-start.1 = (bf16[1,16,8192]{2,1,0:T(8,128)(2,1)S(1)}, bf16[1,16,8192]{2,1,0:T(8,128)(2,1)}, u32[]{:S(2)}) copy-start(bf16[1,16,8192]{2,1,0:T(8,128)(2,1)} %param.11) | copy-start | bytes 786436
  114.7 105.0 %all-gather.4.cloned.1.call-start = ((), (), s32[]{:S(2)}) async-start(), calls=%async_computation.2 | async-start | bytes 4456448 | tf_op jit(solution)/shard_map/all_gather | solution.py:160
  220.8 11.3 %collective-permute-start = (bf16[16,8192]{1,0:T(8,128)(2,1)S(1)}, bf16[16,8192]{1,0:T(8,128)(2,1)S(1)}, u32[]{:S(2)}, u32[]{:S(2)}) collective-permute-start(bf16[16,8192]{1,0:T(8,128)(2,1)S(1)} %fusion.27), channel_id=1, source_target_pairs={{0,16},{16,32},{32,48},{48,64},{64,80},{80,96},{96,112},{112,0},{1... | collective-permute-start | bytes 786440 | tf_op jit(solution)/shard_map/ppermute | solution.py:15
Sparse Core Ops, SparseCore 0:
  9.1 41.0 all-gather.5
  114.8 62.6 reduce-scatter.1
  179.4 40.2 all-gather.3
where the time goes:
time: 240 us; the launch traced here: 239 us
  waiting for transfers between devices  142 us (59%)
  matrix products  45.3 us (19%)
  other arithmetic  24.3 us (10%)
  between operations  14 us (6%)
  local copies, waits for them, and re-layouts  12.6 us (5%)
    reduce_scatter x1, waiting for transfers between devices, local(): lax.psum_scatter(codes8.astype(jnp.bfloat16), 'tp', scatter_dimension=1,...  62.4 us
    all_gather x1, waiting for transfers between devices, local(): whole_shares = lax.all_gather(codes4, 'tp', axis=1, tiled=True)  39.5 us
    all_gather x1, waiting for transfers between devices, local(): lax.all_gather(input_codes[0], 'tp', axis=0, tiled=True).astype(jnp.float32)  29.1 us
    reduce_sum x1, other arithmetic, one_block(): jnp.sum(old_weights, axis=-1, keepdims=True)  15 us
    dot_general x1, matrix products, one_block(): jnp.einsum('hqk,kd->qhd', old_weights, cache_values, preferred_element_ty...  14.9 us
    dot_general x1, matrix products, one_block(): jnp.einsum('qhd,kd->hqk', query_block, cache_keys, preferred_element_type...  13.3 us
    dot_general x1, local copies, waits for them, and re-layouts, local(): jnp.dot(normed, query_weight, preferred_element_type=jnp.float32)  12 us
    ppermute x1, waiting for transfers between devices, shifted(): return lax.ppermute(value, axis, pairs)  9.96 us
  transfers between devices with their start and end apart: 4, of which 4 were waited for; matrix products, arithmetic and copies ran while one was open for 6% of the time, Pallas kernels for 0%

commit v1 on v0

v1 whole, which is shorter than its diff:
```python
import functools
import math

import jax
import jax.numpy as jnp
import numpy as np
from jax import lax
from jax.experimental import pallas as pl
from jax.experimental.pallas import tpu as pltpu
from jax.sharding import PartitionSpec as P

EPSILON = 1e-05
ROPE_BASE = 500000.0
MESH = pl.DeviceIdType.MESH
BF = jnp.bfloat16
F32 = jnp.float32

SECTIONS = 8
D = 8192
HD = 128
HEADS = 4
ROWS = 16
BLOCK = 128
TOKENS = 256
PREFIX = 8192
LEAST = 2048
KC = 1024
NK = D // KC
HALF = D // 2
JC = 1024
NJ = HALF // JC
KEYS = 1024

AG_SEMS = 14
RS_SEMS = 8


def dot(a, b):
    return jnp.dot(a, b, preferred_element_type=F32)


def dot_t(a, b):
    return lax.dot_general(a, b, (((1,), (1,)), ((), ())), preferred_element_type=F32)


def token_of(row):
    return (((row % BLOCK) // ROWS) * 2 + row // BLOCK) * ROWS + row % ROWS


def kernel(
    codes,
    in_exps,
    prefix_len,
    gain,
    freqs,
    wq_hbm,
    wkv_hbm,
    wo_hbm,
    kv_hbm,
    part_exps,
    share_exps,
    out_exps,
    out,
    gathered,
    wq,
    wkv,
    wo,
    kv,
    keys,
    tables,
    acc,
    cosine,
    sine,
    queries,
    new_keys,
    new_values,
    attended,
    partial,
    from_sib,
    sums,
    from_x,
    from_z1,
    from_z2,
    outgoing,
    sib_codes,
    load_sem,
    ag_send,
    ag_recv,
    rs_send,
    rs_recv,
    code_sem,
    pp_send,
    pp_recv,
):
    section = lax.axis_index("pp")
    rank = lax.axis_index("tp")
    core = rank % 2
    z = (rank // 2) % 4
    x = rank // 8
    other = 1 - core
    ox = 1 - x
    zn = (z + 1) % 4
    zp = (z + 3) % 4
    zo = (z + 2) % 4

    def device(xx, zz, cc, steps=0):
        return {"pp": (section + steps) % SECTIONS, "tp": (xx * 4 + zz) * 2 + cc}

    to_next = device(x, zn, core)
    to_prev = device(x, zp, core)
    to_x = device(ox, z, core)
    to_sib = device(x, z, other)

    barrier = pltpu.get_barrier_semaphore()
    greeted = [to_next, to_prev, to_x, to_sib]
    for steps in (1, SECTIONS - 1):
        for cc in (core, other):
            greeted.append(device(x, z, cc, steps))
    for peer in greeted:
        pl.semaphore_signal(barrier, inc=1, device_id=peer, device_id_type=MESH)

    loads = [
        pltpu.make_async_copy(src, dst, load_sem.at[i])
        for i, (src, dst) in enumerate(
            ((wq_hbm, wq), (wkv_hbm, wkv), (kv_hbm, kv), (wo_hbm, wo))
        )
    ]
    for load in loads:
        load.start()

    @pl.loop(0, D // HD // 8)
    def _(chunk):
        for inner in range(8):
            group = chunk * 8 + inner
            cols = pl.ds(pl.multiple_of(group * HD, HD), HD)

            def put(row, exponent):
                value = jnp.full((1, HD), jnp.left_shift(1, exponent + 16), jnp.int32)
                tables[row : row + 1, cols] = value.astype(F32) * (2.0**-16)

            part = part_exps[0, group]
            share = share_exps[0, group]
            outer = out_exps[section, group]
            put(0, in_exps[0, group])
            put(1, -part)
            put(2, part - share)
            put(3, share)
            put(4, -outer)
            put(5, outer)

    own_row = pl.multiple_of(core * BLOCK + (x * 4 + z) * ROWS, ROWS)
    power = jnp.zeros((ROWS, 1), F32)
    for k in range(NK):
        cols = slice(k * KC, (k + 1) * KC)
        resid = codes[:, cols].astype(F32) * tables[0:1, cols]
        power = power + jnp.sum(resid * resid, axis=1, keepdims=True)
    inverse = lax.rsqrt(power * (1.0 / D) + EPSILON)
    for k in range(NK):
        cols = slice(k * KC, (k + 1) * KC)
        resid = codes[:, cols].astype(F32) * tables[0:1, cols]
        gathered[k, pl.ds(own_row, ROWS), :] = (
            resid * inverse * gain[:, cols].astype(F32)
        ).astype(BF)

    pl.semaphore_wait(barrier, len(greeted))

    pending = []

    def remote(src, dst, send, recv, peer):
        copy = pltpu.make_async_remote_copy(
            src_ref=src,
            dst_ref=dst,
            send_sem=send,
            recv_sem=recv,
            device_id=peer,
            device_id_type=MESH,
        )
        copy.start()
        pending.append(copy)
        return copy

    sib_cols = pl.ds(pl.multiple_of(other * HALF, HALF), HALF)
    own_cols = pl.ds(pl.multiple_of(core * HALF, HALF), HALF)
    code_copy = remote(
        codes.at[:, sib_cols], sib_codes, code_sem.at[0], code_sem.at[1], to_sib
    )

    def piece(xx, zz):
        return pl.ds(pl.multiple_of(core * BLOCK + (xx * 4 + zz) * ROWS, ROWS), ROWS)

    full = slice(0, KC)
    low = slice(0, KC // 2)
    high = slice(KC // 2, KC)
    copies = {}

    def share(k, slot, rows, cols, peer):
        ref = gathered.at[k, rows, cols]
        copies[k, slot] = remote(ref, ref, ag_send.at[k, slot], ag_recv.at[k, slot], peer)

    def arrived(k, *slots):
        for slot in slots:
            copies[k, slot].wait_recv()

    def x_rows(xx):
        return pl.ds(pl.multiple_of(core * BLOCK + xx * (BLOCK // 2), BLOCK // 2), BLOCK // 2)

    def gather_stage(stage, k):
        z_first = k % 2 == 0
        if stage == 0:
            share(k, 0, piece(x, z), full, to_x)
            share(k, 1, piece(x, z), full, to_next)
            share(k, 2, piece(x, z), full, to_prev)
        elif z_first and stage == 1:
            arrived(k, 1, 2)
            share(k, 3, piece(x, zp), low, to_next)
            share(k, 4, piece(x, zn), high, to_prev)
            share(k, 5, piece(x, zp), full, to_x)
            share(k, 6, piece(x, zn), full, to_x)
        elif z_first and stage == 2:
            arrived(k, 3, 4)
            share(k, 7, piece(x, zo), full, to_x)
            share(k, 8, x_rows(x), full, to_sib)
        elif z_first and stage == 3:
            arrived(k, 0, 5, 6, 7)
            share(k, 9, x_rows(ox), full, to_sib)
        elif z_first and stage == 4:
            arrived(k, 8, 9)
        elif stage == 1:
            arrived(k, 0)
            share(k, 3, piece(ox, z), full, to_next)
            share(k, 4, piece(ox, z), full, to_prev)
        elif stage == 2:
            arrived(k, 1, 2, 3, 4)
            share(k, 5, piece(x, zp), low, to_next)
            share(k, 6, piece(ox, zp), low, to_next)
            share(k, 7, piece(x, zn), high, to_prev)
            share(k, 8, piece(ox, zn), high, to_prev)
        elif stage == 3:
            arrived(k, 5, 6, 7, 8)
            rows = pl.ds(pl.multiple_of(core * BLOCK, BLOCK), BLOCK)
            share(k, 9, rows, full, to_sib)
        else:
            arrived(k, 9)

    def project(k):
        rows = gathered[k]
        cols = slice(k * KC, (k + 1) * KC)
        if k == 0:
            acc[:, : HEADS * HD] = dot(rows, wq[cols, :])
            acc[:, HEADS * HD :] = dot(rows, wkv[cols, :])
        else:
            acc[:, : HEADS * HD] += dot(rows, wq[cols, :])
            acc[:, HEADS * HD :] += dot(rows, wkv[cols, :])

    length = prefix_len[0]

    def make_rotary():
        row = lax.broadcasted_iota(jnp.int32, (TOKENS, HD), 0)
        angle = (length + token_of(row)).astype(F32) * freqs[...]
        lane = lax.broadcasted_iota(jnp.int32, (TOKENS, HD), 1)
        cosine[...] = jnp.cos(angle)
        sine[...] = jnp.where(lane < HD // 2, -1.0, 1.0) * jnp.sin(angle)

    def make_keys():
        first = kv[0:ROWS, :HD][0:1, :]

        @pl.loop(0, PREFIX // 1024)
        def _(chunk):
            start = pl.multiple_of(chunk * 1024, 1024)
            rows = pl.ds(start, 1024)
            position = lax.broadcasted_iota(jnp.int32, (1024, HD), 0) + start
            live = position < length
            keys[rows, :] = jnp.where(live, kv[rows, :HD], first)
            kv[rows, HD:] = jnp.where(live, kv[rows, HD:], jnp.zeros((), BF))
            kv[rows, :HD] = jnp.where(live, 1.0, 0.0).astype(BF)

    LEAD = 2
    for tick in range(-LEAD, NK + 4):
        if tick + LEAD < NK:
            gather_stage(0, tick + LEAD)
        for stage in (1, 2, 3, 4):
            k = tick - stage + 1
            if 0 <= k < NK:
                gather_stage(stage, k)
        if tick == 0:
            make_rotary()
        if tick == 2:
            loads[2].wait()
            make_keys()
        if tick == 3:
            loads[0].wait()
            loads[1].wait()
        if 0 <= tick - 3 < NK:
            project(tick - 3)

    q_scale = math.log2(math.e) / math.sqrt(HD)

    def rotated(cols):
        value = acc[:, cols]
        return value * cosine[...] + pltpu.roll(value, HD // 2, 1) * sine[...]

    for head in range(HEADS):
        value = (rotated(slice(head * HD, (head + 1) * HD)) * q_scale).astype(BF)
        for block in range(2):
            queries[block, head * BLOCK : (head + 1) * BLOCK, :] = value[
                block * BLOCK : (block + 1) * BLOCK
            ]
    base = HEADS * HD
    new_keys[...] = rotated(slice(base, base + HD)).astype(BF)
    new_values[:, HD:] = acc[:, base + HD :].astype(BF)
    new_values[:, :HD] = jnp.ones((TOKENS, HD), BF)

    def attend(block, after):
        state = []
        row = lax.broadcasted_iota(jnp.int32, (BLOCK, TOKENS), 0) + block * BLOCK
        col = lax.broadcasted_iota(jnp.int32, (BLOCK, TOKENS), 1)
        seen = token_of(col) <= token_of(row)
        for head in range(HEADS):
            q = queries[block, head * BLOCK : (head + 1) * BLOCK, :]
            score = jnp.where(seen, dot_t(q, new_keys[...]), -1e30)
            top = jnp.max(score, axis=1, keepdims=True)
            weight = jnp.exp2(score - top).astype(BF)
            state.append((top, dot(weight, new_values[...])))
        for chunk in range(PREFIX // KEYS):
            rows = slice(chunk * KEYS, (chunk + 1) * KEYS)
            for head in range(HEADS):
                top, total = state[head]
                q = queries[block, head * BLOCK : (head + 1) * BLOCK, :]
                score = dot_t(q, keys[rows, :])
                new_top = jnp.maximum(top, jnp.max(score, axis=1, keepdims=True))
                weight = jnp.exp2(score - new_top).astype(BF)
                total = total * jnp.exp2(top - new_top) + dot(weight, kv[rows, :])
                state[head] = (new_top, total)
            after(chunk)
        for head in range(HEADS):
            total = state[head][1]
            attended[block, :, head * HD : (head + 1) * HD] = (
                total[:, HD:] / total[:, :HD]
            ).astype(BF)

    def half_cols(which, j):
        return pl.ds(pl.multiple_of(which * HALF + j * JC, JC), JC)

    def out_project(block, which, j):
        cols = half_cols(which, j)
        value = dot(attended[block], wo[:, cols]) * tables[1:2, cols]
        return jnp.clip(value, -127.0, 127.0).astype(BF)

    rs = {}

    def hand(block, j, slot, src, dst, peer):
        sem = block * NJ + j
        rs[block, j, slot] = remote(src, dst, rs_send.at[sem, slot], rs_recv.at[sem, slot], peer)

    def got(block, j, *slots):
        for slot in slots:
            rs[block, j, slot].wait_recv()

    def z_rows(zz):
        return pl.ds(pl.multiple_of(zz * ROWS, ROWS), ROWS)

    lo = slice(0, JC // 2)
    hi = slice(JC // 2, JC)

    def add(*values):
        total = values[0].astype(F32)
        for value in values[1:]:
            total = total + value.astype(F32)
        return total

    def produce(block, j):
        partial[block, j] = out_project(block, other, j)
        hand(block, j, 0, partial.at[block, j], from_sib.at[block, j], to_sib)
        sums[block, j] = out_project(block, core, j).reshape(2, BLOCK // 2, JC)

    def finish(block, j, total):
        cols = half_cols(core, j)
        is_own = core == block
        own = codes[:, cols]
        sib = sib_codes[:, j * JC : (j + 1) * JC]
        resid = jnp.where(is_own, own.astype(F32), sib.astype(F32)) * row_scale(block, cols)
        codes4 = jnp.clip(total * tables[2:3, cols], -7.0, 7.0).astype(BF)
        updated = resid + codes4.astype(F32) * tables[3:4, cols]
        coded = jnp.clip(updated * tables[4:5, cols], -127.0, 127.0).astype(BF)
        outgoing[block, j] = (coded.astype(F32) * tables[5:6, cols]).astype(BF)
        slot = core * NJ + j
        remote(
            outgoing.at[block, j],
            out.at[:, cols],
            pp_send.at[block, j],
            pp_recv.at[slot],
            device(x, z, block, 1),
        )

    def row_scale(block, cols):
        return tables[0:1, cols]

    def reduce_stage(stage, block, j):
        ref = sums.at[block, j]
        z_first = j >= NJ // 2
        if stage == 0:
            got(block, j, 0)
            for part in range(2):
                rows = slice(part * (BLOCK // 2), (part + 1) * (BLOCK // 2))
                ref[part] = add(ref[part], from_sib[block, j, rows, :]).astype(BF)
            if z_first:
                hand(block, j, 1, ref.at[:, z_rows(zo), lo], from_z1.at[block, j, 0], to_next)
                hand(block, j, 2, ref.at[:, z_rows(zo), hi], from_z1.at[block, j, 1], to_prev)
            else:
                hand(block, j, 1, ref.at[ox], from_x.at[block, j], to_x)
        elif z_first and stage == 1:
            got(block, j, 1, 2)
            ref[:, z_rows(zn), lo] = add(ref[:, z_rows(zn), lo], from_z1[block, j, 0]).astype(BF)
            ref[:, z_rows(zp), hi] = add(ref[:, z_rows(zp), hi], from_z1[block, j, 1]).astype(BF)
            hand(block, j, 3, ref.at[:, z_rows(zn), :], from_z2.at[block, j, 0], to_next)
            hand(block, j, 4, ref.at[:, z_rows(zp), :], from_z2.at[block, j, 1], to_prev)
        elif z_first and stage == 2:
            got(block, j, 3, 4)
            ref[:, z_rows(z), :] = add(
                ref[:, z_rows(z), :], from_z2[block, j, 0], from_z2[block, j, 1]
            ).astype(BF)
            hand(
                block,
                j,
                5,
                ref.at[ox, z_rows(z), :],
                from_x.at[block, j, 0:ROWS, :],
                to_x,
            )
        elif z_first:
            got(block, j, 5)
            finish(block, j, add(ref[x, z_rows(z), :], from_x[block, j, 0:ROWS, :]))
        elif stage == 1:
            got(block, j, 1)
            ref[x] = add(ref[x], from_x[block, j]).astype(BF)
            hand(block, j, 2, ref.at[x, z_rows(zo), lo], from_z1.at[block, j, 0, 0], to_next)
            hand(block, j, 3, ref.at[x, z_rows(zo), hi], from_z1.at[block, j, 1, 0], to_prev)
        elif stage == 2:
            got(block, j, 2, 3)
            ref[x, z_rows(zn), lo] = add(ref[x, z_rows(zn), lo], from_z1[block, j, 0, 0]).astype(BF)
            ref[x, z_rows(zp), hi] = add(ref[x, z_rows(zp), hi], from_z1[block, j, 1, 0]).astype(BF)
            hand(block, j, 4, ref.at[x, z_rows(zn), :], from_z2.at[block, j, 0, 0], to_next)
            hand(block, j, 5, ref.at[x, z_rows(zp), :], from_z2.at[block, j, 1, 0], to_prev)
        else:
            got(block, j, 4, 5)
            finish(
                block,
                j,
                add(ref[x, z_rows(z), :], from_z2[block, j, 0, 0], from_z2[block, j, 1, 0]),
            )

    code_copy.wait_recv()
    attend(0, lambda chunk: None)
    loads[3].wait()

    def steps_of(block):
        return [(0, 2), (1, 2), (0, 3), (1, 3), (2, 2), (1, 0), (2, 3), (3, 2), (1, 1), (2, 0), (3, 3), (2, 1), (3, 0), (3, 1)]

    def run_produce(block):
        for j in range(NJ):
            produce(block, j)
            if j >= 1:
                if j - 1 < NJ // 2:
                    reduce_stage(0, block, j - 1)

    run_produce(0)
    todo = [(stage, 0, j) for stage, j in steps_of(0)]

    def serve(chunk):
        for _ in range(2):
            if todo:
                reduce_stage(*todo.pop(0))

    attend(1, serve)
    run_produce(1)
    for item in todo:
        reduce_stage(*item)
    for stage, j in steps_of(1):
        reduce_stage(stage, 1, j)

    for which in range(2):
        for j in range(NJ):
            ref = out.at[:, pl.ds(which * HALF + j * JC, JC)]
            pltpu.make_async_copy(ref, ref, pp_recv.at[which * NJ + j]).wait()
    for copy in pending:
        copy.wait_send()


def local(
    input_codes,
    input_exps,
    prefix_len,
    norm_gain,
    w_query,
    w_keyval,
    w_out,
    kv_cache,
    partial_exps,
    share_exps,
    output_exps,
):
    half = np.power(np.float64(ROPE_BASE), -2.0 * np.arange(HD // 2) / HD).astype(np.float32)
    freqs = jnp.asarray(np.concatenate([half, half])[None, :])
    vmem = pl.BlockSpec(memory_space=pltpu.VMEM)
    smem = pl.BlockSpec(memory_space=pltpu.SMEM)
    hbm = pl.BlockSpec(memory_space=pl.ANY)
    dma = pltpu.SemaphoreType.DMA
    scratch = [
        pltpu.VMEM((NK, TOKENS, KC), BF),
        pltpu.VMEM((D, HEADS * HD), BF),
        pltpu.VMEM((D, 2 * HD), BF),
        pltpu.VMEM((HEADS * HD, D), BF),
        pltpu.VMEM((PREFIX, 2 * HD), BF),
        pltpu.VMEM((PREFIX, HD), BF),
        pltpu.VMEM((8, D), F32),
        pltpu.VMEM((TOKENS, (HEADS + 2) * HD), F32),
        pltpu.VMEM((TOKENS, HD), F32),
        pltpu.VMEM((TOKENS, HD), F32),
        pltpu.VMEM((2, HEADS * BLOCK, HD), BF),
        pltpu.VMEM((TOKENS, HD), BF),
        pltpu.VMEM((TOKENS, 2 * HD), BF),
        pltpu.VMEM((2, BLOCK, HEADS * HD), BF),
        pltpu.VMEM((2, NJ, BLOCK, JC), BF),
        pltpu.VMEM((2, NJ, BLOCK, JC), BF),
        pltpu.VMEM((2, NJ, 2, BLOCK // 2, JC), BF),
        pltpu.VMEM((2, NJ, BLOCK // 2, JC), BF),
        pltpu.VMEM((2, NJ, 2, 2, ROWS, JC // 2), BF),
        pltpu.VMEM((2, NJ, 2, 2, ROWS, JC), BF),
        pltpu.VMEM((2, NJ, ROWS, JC), BF),
        pltpu.VMEM((ROWS, HALF), BF),
        dma((4,)),
        dma((NK, 10)),
        dma((NK, 10)),
        dma((2 * NJ, 6)),
        dma((2 * NJ, 6)),
        dma((2,)),
        dma((2, NJ)),
        dma((2 * NJ,)),
    ]
    received = pl.pallas_call(
        kernel,
        out_shape=jax.ShapeDtypeStruct((ROWS, D), BF),
        in_specs=[vmem, smem, smem, vmem, vmem, hbm, hbm, hbm, hbm, smem, smem, smem],
        out_specs=hbm,
        scratch_shapes=scratch,
        compiler_params=pltpu.CompilerParams(
            collective_id=1, has_side_effects=True, vmem_limit_bytes=60 * 2**20
        ),
        cost_estimate=pl.CostEstimate(
            flops=10 * 10**9, bytes_accessed=26 * 2**20, transcendentals=9 * 10**6
        ),
        name="relay_section",
    )(
        input_codes[0],
        input_exps,
        prefix_len,
        norm_gain,
        freqs,
        w_query[0],
        w_keyval.reshape(D, 2 * HD),
        w_out[0],
        kv_cache.reshape(PREFIX, 2 * HD),
        partial_exps,
        share_exps,
        output_exps,
    )
    return received[None]


def solution(mesh):
    in_specs = (
        P("pp", "tp", None),
        P("pp", None),
        P("pp"),
        P("pp", None),
        P("pp", None, "tp"),
        P("pp", None, "tp", None),
        P("pp", "tp", None),
        P("pp", "tp", None, None),
        P("pp", None),
        P("pp", None),
        P(),
    )
    out_specs = P("pp", "tp", None)
    return jax.shard_map(local, mesh=mesh, in_specs=in_specs, out_specs=out_specs, check_vma=False)
```

time: 240 us -> 104 us (0.43)
  waiting for transfers between devices: 142 us -> 0 us
  Pallas kernels: 0 us -> 102 us
  matrix products: 45.3 us -> 0 us
  other arithmetic: 24.3 us -> 0 us
  between operations: 14 us -> 0.66 us
  local copies, waits for them, and re-layouts: 12.6 us -> 1.67 us
    pallas_call x0 -> x1, Pallas kernels: none -> 102 us  [local(): pl.pallas_call(kernel, out_shape=jax.ShapeDtypeStruct((ROWS, D), BF), in_...]
    all_gather x2 -> x0, waiting for transfers between devices: 68.6 us -> none  [the longest x1 39.5 us: local(): whole_shares = lax.all_gather(codes4, 'tp', axis=1, tiled=True)]
    reduce_scatter x1 -> x0, waiting for transfers between devices: 62.4 us -> none  [local(): lax.psum_scatter(codes8.astype(jnp.bfloat16), 'tp', scatter_dimension=1,...]
    dot_general x7 -> x0, matrix products: 45.3 us -> none  [the longest x1 14.9 us: one_block(): jnp.einsum('hqk,kd->qhd', old_weights, cache_values, preferred_element_ty...]
    reduce_sum x3 -> x0, other arithmetic: 18.7 us -> none  [the longest x1 15 us: one_block(): jnp.sum(old_weights, axis=-1, keepdims=True)]
    dot_general x1 -> x0, local copies, waits for them, and re-layouts: 12 us -> none  [local(): jnp.dot(normed, query_weight, preferred_element_type=jnp.float32)]
    ppermute x1 -> x0, waiting for transfers between devices: 9.96 us -> none  [shifted(): return lax.ppermute(value, axis, pairs)]
    convert_element_type x3 -> x0, other arithmetic: 2.82 us -> none  [the longest x1 1.73 us: local(): jnp.clip(total * own_part * own_inverse, -7.0, 7.0).astype(jnp.bfloat16)]
  transfers between devices with their start and end apart: 4 -> 0, of which waited for: 4 -> 0; matrix products, arithmetic and copies ran while one was open for 6% -> 0% of each run, Pallas kernels for 0% -> 0%
where the time goes in v1:
time: 104 us
  Pallas kernels  102 us (98%)
  local copies, waits for them, and re-layouts  1.67 us (2%)
    pallas_call x1, Pallas kernels, local(): pl.pallas_call(kernel, out_shape=jax.ShapeDtypeStruct((ROWS, D), BF), in_...  102 us

profile of v1, /device:TPU:1, one launch (start us, length us, event | category | flops | bytes accessed | tf_op | source)
XLA Modules:
  0.0 104.3 jit_solution(13606629907567261279)
XLA Ops:
  0.7 102.0 %relay_section.1 = bf16[16,8192]{1,0:T(8,128)(2,1)} custom-call(bf16[16,8192]{1,0:T(8,128)(2,1)} %bitcast.11, s32[1,64]{1,0:T(1,128)} %in_exps.1, s32[1]{0:T(128)S(6)} %copy.14.prefix_len, bf16[1,8192]{1,0:T(2,128)(2,1)} %gain.1, f32[1,128]{1,0:T(1,128)} %constant.2.clone.freqs, bf16[8192,512]{1,0:T(8,128)(2,1)} %bitcast.7, bf16[8192,256]{1,0:T(8,128)(2,1)} %bitcast.9, ...), custom_call_target="tpu_custom_call" | custom-call | flops 10000000000 | bytes 27262976 | tf_op jit(solution)/shard_map/relay_section/pallas_call | solution.py:540
  102.6 1.7 %copy.15 = bf16[1,16,8192]{2,1,0:T(8,128)(2,1)} copy(bf16[1,16,8192]{2,1,0:T(8,128)(2,1)} %bitcast.6) | data formatting | bytes 524288

commit v2 on v1

--- a/solution.py
+++ b/solution.py
@@ -31,8 +31,8 @@
 NJ = HALF // JC
 KEYS = 1024
 
-AG_SEMS = 14
-RS_SEMS = 8
+Z_FIRST = "zxzxzxzx"
+X_REDUCE = "xzxz"
 
 
 def dot(a, b):
@@ -79,8 +79,7 @@
     from_sib,
     sums,
     from_x,
-    from_z1,
-    from_z2,
+    from_z,
     outgoing,
     sib_codes,
     load_sem,
@@ -108,14 +107,14 @@
 
     to_next = device(x, zn, core)
     to_prev = device(x, zp, core)
+    to_far = device(x, zo, core)
     to_x = device(ox, z, core)
     to_sib = device(x, z, other)
 
     barrier = pltpu.get_barrier_semaphore()
-    greeted = [to_next, to_prev, to_x, to_sib]
-    for steps in (1, SECTIONS - 1):
-        for cc in (core, other):
-            greeted.append(device(x, z, cc, steps))
+    greeted = [to_next, to_prev, to_far, to_x, to_sib]
+    for cc in (core, other):
+        greeted.append(device(x, z, cc, SECTIONS - 1))
     for peer in greeted:
         pl.semaphore_signal(barrier, inc=1, device_id=peer, device_id_type=MESH)
 
@@ -205,7 +204,7 @@
         return pl.ds(pl.multiple_of(core * BLOCK + xx * (BLOCK // 2), BLOCK // 2), BLOCK // 2)
 
     def gather_stage(stage, k):
-        z_first = k % 2 == 0
+        z_first = Z_FIRST[k] == "z"
         if stage == 0:
             share(k, 0, piece(x, z), full, to_x)
             share(k, 1, piece(x, z), full, to_next)
@@ -274,24 +273,29 @@
             kv[rows, HD:] = jnp.where(live, kv[rows, HD:], jnp.zeros((), BF))
             kv[rows, :HD] = jnp.where(live, 1.0, 0.0).astype(BF)
 
-    LEAD = 2
-    for tick in range(-LEAD, NK + 4):
-        if tick + LEAD < NK:
-            gather_stage(0, tick + LEAD)
-        for stage in (1, 2, 3, 4):
-            k = tick - stage + 1
-            if 0 <= k < NK:
-                gather_stage(stage, k)
-        if tick == 0:
-            make_rotary()
-        if tick == 2:
-            loads[2].wait()
-            make_keys()
-        if tick == 3:
-            loads[0].wait()
-            loads[1].wait()
-        if 0 <= tick - 3 < NK:
-            project(tick - 3)
+    for k in range(NK):
+        gather_stage(0, k)
+    make_rotary()
+    for k in range(NK // 2):
+        gather_stage(1, k)
+    loads[2].wait()
+    make_keys()
+    for k in range(NK // 2, NK):
+        gather_stage(1, k)
+        gather_stage(2, k - NK // 2)
+    loads[0].wait()
+    loads[1].wait()
+    for k in range(NK // 2, NK):
+        gather_stage(2, k)
+        gather_stage(3, k - NK // 2)
+    for k in range(NK // 2, NK + 1):
+        if k < NK:
+            gather_stage(3, k)
+        gather_stage(4, k - NK // 2)
+        project(k - NK // 2)
+    for k in range(NK // 2 + 1, NK):
+        gather_stage(4, k)
+        project(k)
 
     q_scale = math.log2(math.e) / math.sqrt(HD)
 
@@ -359,9 +363,6 @@
     def z_rows(zz):
         return pl.ds(pl.multiple_of(zz * ROWS, ROWS), ROWS)
 
-    lo = slice(0, JC // 2)
-    hi = slice(JC // 2, JC)
-
     def add(*values):
         total = values[0].astype(F32)
         for value in values[1:]:
@@ -395,88 +396,62 @@
     def row_scale(block, cols):
         return tables[0:1, cols]
 
+    across = ((0, zn, to_next), (1, zp, to_prev), (2, zo, to_far))
+
     def reduce_stage(stage, block, j):
         ref = sums.at[block, j]
-        z_first = j >= NJ // 2
+        x_first = X_REDUCE[j] == "x"
         if stage == 0:
             got(block, j, 0)
             for part in range(2):
                 rows = slice(part * (BLOCK // 2), (part + 1) * (BLOCK // 2))
                 ref[part] = add(ref[part], from_sib[block, j, rows, :]).astype(BF)
-            if z_first:
-                hand(block, j, 1, ref.at[:, z_rows(zo), lo], from_z1.at[block, j, 0], to_next)
-                hand(block, j, 2, ref.at[:, z_rows(zo), hi], from_z1.at[block, j, 1], to_prev)
+            if x_first:
+                hand(block, j, 1, ref.at[ox], from_x.at[block, j], to_x)
             else:
-                hand(block, j, 1, ref.at[ox], from_x.at[block, j], to_x)
-        elif z_first and stage == 1:
-            got(block, j, 1, 2)
-            ref[:, z_rows(zn), lo] = add(ref[:, z_rows(zn), lo], from_z1[block, j, 0]).astype(BF)
-            ref[:, z_rows(zp), hi] = add(ref[:, z_rows(zp), hi], from_z1[block, j, 1]).astype(BF)
-            hand(block, j, 3, ref.at[:, z_rows(zn), :], from_z2.at[block, j, 0], to_next)
-            hand(block, j, 4, ref.at[:, z_rows(zp), :], from_z2.at[block, j, 1], to_prev)
-        elif z_first and stage == 2:
-            got(block, j, 3, 4)
-            ref[:, z_rows(z), :] = add(
-                ref[:, z_rows(z), :], from_z2[block, j, 0], from_z2[block, j, 1]
-            ).astype(BF)
-            hand(
-                block,
-                j,
-                5,
-                ref.at[ox, z_rows(z), :],
-                from_x.at[block, j, 0:ROWS, :],
-                to_x,
-            )
-        elif z_first:
-            got(block, j, 5)
-            finish(block, j, add(ref[x, z_rows(z), :], from_x[block, j, 0:ROWS, :]))
-        elif stage == 1:
+                for slot, zz, peer in across:
+                    hand(block, j, 1 + slot, ref.at[:, z_rows(zz), :], from_z.at[block, j, slot], peer)
+        elif x_first and stage == 1:
             got(block, j, 1)
             ref[x] = add(ref[x], from_x[block, j]).astype(BF)
-            hand(block, j, 2, ref.at[x, z_rows(zo), lo], from_z1.at[block, j, 0, 0], to_next)
-            hand(block, j, 3, ref.at[x, z_rows(zo), hi], from_z1.at[block, j, 1, 0], to_prev)
-        elif stage == 2:
-            got(block, j, 2, 3)
-            ref[x, z_rows(zn), lo] = add(ref[x, z_rows(zn), lo], from_z1[block, j, 0, 0]).astype(BF)
-            ref[x, z_rows(zp), hi] = add(ref[x, z_rows(zp), hi], from_z1[block, j, 1, 0]).astype(BF)
-            hand(block, j, 4, ref.at[x, z_rows(zn), :], from_z2.at[block, j, 0, 0], to_next)
-            hand(block, j, 5, ref.at[x, z_rows(zp), :], from_z2.at[block, j, 1, 0], to_prev)
+            for slot, zz, peer in across:
+                hand(block, j, 2 + slot, ref.at[x, z_rows(zz), :], from_z.at[block, j, slot, 0], peer)
+        elif x_first:
+            got(block, j, 2, 3, 4)
+            parts = [from_z[block, j, slot, 0] for slot in range(3)]
+            finish(block, j, add(ref[x, z_rows(z), :], *parts))
+        elif stage == 1:
+            got(block, j, 1, 2, 3)
+            parts = [from_z[block, j, slot] for slot in range(3)]
+            ref[:, z_rows(z), :] = add(ref[:, z_rows(z), :], *parts).astype(BF)
+            hand(block, j, 4, ref.at[ox, z_rows(z), :], from_x.at[block, j, 0:ROWS, :], to_x)
         else:
-            got(block, j, 4, 5)
-            finish(
-                block,
-                j,
-                add(ref[x, z_rows(z), :], from_z2[block, j, 0, 0], from_z2[block, j, 1, 0]),
-            )
+            got(block, j, 4)
+            finish(block, j, add(ref[x, z_rows(z), :], from_x[block, j, 0:ROWS, :]))
 
     code_copy.wait_recv()
     attend(0, lambda chunk: None)
     loads[3].wait()
 
-    def steps_of(block):
-        return [(0, 2), (1, 2), (0, 3), (1, 3), (2, 2), (1, 0), (2, 3), (3, 2), (1, 1), (2, 0), (3, 3), (2, 1), (3, 0), (3, 1)]
-
-    def run_produce(block):
+    def run_produce(block, after):
         for j in range(NJ):
             produce(block, j)
             if j >= 1:
-                if j - 1 < NJ // 2:
-                    reduce_stage(0, block, j - 1)
-
-    run_produce(0)
-    todo = [(stage, 0, j) for stage, j in steps_of(0)]
+                reduce_stage(0, block, j - 1)
+            after(j)
+        reduce_stage(0, block, NJ - 1)
 
     def serve(chunk):
-        for _ in range(2):
-            if todo:
-                reduce_stage(*todo.pop(0))
-
+        if chunk >= 4:
+            reduce_stage(1, 0, chunk - 4)
+
+    run_produce(0, lambda j: None)
     attend(1, serve)
-    run_produce(1)
-    for item in todo:
-        reduce_stage(*item)
-    for stage, j in steps_of(1):
-        reduce_stage(stage, 1, j)
+    run_produce(1, lambda j: reduce_stage(2, 0, j))
+    for j in range(NJ):
+        reduce_stage(1, 1, j)
+    for j in range(NJ):
+        reduce_stage(2, 1, j)
 
     for which in range(2):
         for j in range(NJ):
@@ -524,8 +499,7 @@
         pltpu.VMEM((2, NJ, BLOCK, JC), BF),
         pltpu.VMEM((2, NJ, 2, BLOCK // 2, JC), BF),
         pltpu.VMEM((2, NJ, BLOCK // 2, JC), BF),
-        pltpu.VMEM((2, NJ, 2, 2, ROWS, JC // 2), BF),
-        pltpu.VMEM((2, NJ, 2, 2, ROWS, JC), BF),
+        pltpu.VMEM((2, NJ, 3, 2, ROWS, JC), BF),
         pltpu.VMEM((2, NJ, ROWS, JC), BF),
         pltpu.VMEM((ROWS, HALF), BF),
         dma((4,)),

time: 104 us -> 74.6 us (0.72)
  Pallas kernels: 102 us -> 72.1 us
    pallas_call x1, Pallas kernels: 102 us -> 72.1 us  [local(): pl.pallas_call(kernel, out_shape=jax.ShapeDtypeStruct((ROWS, D), BF), in_...]
where the time goes in v2:
time: 74.6 us; the launch traced here: 74.5 us
  Pallas kernels  72.1 us (97%)
  local copies, waits for them, and re-layouts  1.67 us (2%)
    pallas_call x1, Pallas kernels, local(): pl.pallas_call(kernel, out_shape=jax.ShapeDtypeStruct((ROWS, D), BF), in_...  72.1 us
    unnamed x1, local copies, waits for them, and re-layouts  1.67 us

profile of v2, /device:TPU:1, one launch (start us, length us, event | category | flops | bytes accessed | tf_op | source)
XLA Modules:
  0.0 74.5 jit_solution(10978679769541434963)
XLA Ops:
  0.7 72.1 %relay_section.1 = bf16[16,8192]{1,0:T(8,128)(2,1)} custom-call(bf16[16,8192]{1,0:T(8,128)(2,1)} %bitcast.11, s32[1,64]{1,0:T(1,128)} %in_exps.1, s32[1]{0:T(128)S(6)} %copy.14.prefix_len, bf16[1,8192]{1,0:T(2,128)(2,1)} %gain.1, f32[1,128]{1,0:T(1,128)} %constant.2.clone.freqs, bf16[8192,512]{1,0:T(8,128)(2,1)} %bitcast.7, bf16[8192,256]{1,0:T(8,128)(2,1)} %bitcast.9, ...), custom_call_target="tpu_custom_call" | custom-call | flops 10000000000 | bytes 27262976 | tf_op jit(solution)/shard_map/relay_section/pallas_call | solution.py:514
  72.8 1.7 %copy.15 = bf16[1,16,8192]{2,1,0:T(8,128)(2,1)} copy(bf16[1,16,8192]{2,1,0:T(8,128)(2,1)} %bitcast.6) | data formatting | bytes 524288

commit v3 on v2

--- a/solution.py
+++ b/solution.py
@@ -31,7 +31,7 @@
 NJ = HALF // JC
 KEYS = 1024
 
-Z_FIRST = "zxzxzxzx"
+Z_FIRST = "xxxxzzzz"
 X_REDUCE = "xzxz"
 
 
@@ -48,19 +48,27 @@
 
 
 def kernel(
+    codes_hbm,
+    in_exps_hbm,
+    prefix_hbm,
+    gain_hbm,
+    freqs_hbm,
+    wq_hbm,
+    wkv_hbm,
+    wo_hbm,
+    kv_hbm,
+    part_exps_hbm,
+    share_exps_hbm,
+    out_exps_hbm,
+    out,
     codes,
     in_exps,
     prefix_len,
     gain,
     freqs,
-    wq_hbm,
-    wkv_hbm,
-    wo_hbm,
-    kv_hbm,
     part_exps,
     share_exps,
     out_exps,
-    out,
     gathered,
     wq,
     wkv,
@@ -81,13 +89,15 @@
     from_x,
     from_z,
     outgoing,
-    sib_codes,
+    resid_codes,
+    small_sem,
     load_sem,
     ag_send,
     ag_recv,
     rs_send,
     rs_recv,
-    code_sem,
+    code_send_sem,
+    code_recv_sem,
     pp_send,
     pp_recv,
 ):
@@ -101,6 +111,10 @@
     zn = (z + 1) % 4
     zp = (z + 3) % 4
     zo = (z + 2) % 4
+    turned = (section % 4) // 3
+    fx = (x + turned) % 2
+    gx = 1 - fx
+    came_x = (x + ((section + SECTIONS - 1) % 4) // 3) % 2
 
     def device(xx, zz, cc, steps=0):
         return {"pp": (section + steps) % SECTIONS, "tp": (xx * 4 + zz) * 2 + cc}
@@ -111,10 +125,27 @@
     to_x = device(ox, z, core)
     to_sib = device(x, z, other)
 
+    small = [
+        pltpu.make_async_copy(src, dst, small_sem.at[i])
+        for i, (src, dst) in enumerate(
+            (
+                (codes_hbm, codes),
+                (gain_hbm, gain),
+                (in_exps_hbm, in_exps),
+                (part_exps_hbm, part_exps),
+                (share_exps_hbm, share_exps),
+                (out_exps_hbm, out_exps),
+                (prefix_hbm, prefix_len),
+                (freqs_hbm, freqs),
+            )
+        )
+    ]
+    for load in small:
+        load.start()
     barrier = pltpu.get_barrier_semaphore()
-    greeted = [to_next, to_prev, to_far, to_x, to_sib]
+    greeted = [to_next, to_prev, to_far, to_x, to_sib, device(ox, z, other)]
     for cc in (core, other):
-        greeted.append(device(x, z, cc, SECTIONS - 1))
+        greeted.append(device(came_x, z, cc, SECTIONS - 1))
     for peer in greeted:
         pl.semaphore_signal(barrier, inc=1, device_id=peer, device_id_type=MESH)
 
@@ -126,6 +157,9 @@
     ]
     for load in loads:
         load.start()
+
+    for load in small:
+        load.wait()
 
     @pl.loop(0, D // HD // 8)
     def _(chunk):
@@ -178,11 +212,23 @@
         pending.append(copy)
         return copy
 
-    sib_cols = pl.ds(pl.multiple_of(other * HALF, HALF), HALF)
-    own_cols = pl.ds(pl.multiple_of(core * HALF, HALF), HALF)
-    code_copy = remote(
-        codes.at[:, sib_cols], sib_codes, code_sem.at[0], code_sem.at[1], to_sib
-    )
+    def half_of(which):
+        return pl.ds(pl.multiple_of(which * HALF, HALF), HALF)
+
+    def code_send(which, peer):
+        return pltpu.make_async_remote_copy(
+            src_ref=codes.at[:, half_of(which)],
+            dst_ref=resid_codes.at[core],
+            send_sem=code_send_sem.at[which],
+            recv_sem=code_recv_sem.at[core],
+            device_id=peer,
+            device_id_type=MESH,
+        )
+
+    def code_keep():
+        return pltpu.make_async_copy(
+            codes.at[:, half_of(core)], resid_codes.at[core], code_recv_sem.at[core]
+        )
 
     def piece(xx, zz):
         return pl.ds(pl.multiple_of(core * BLOCK + (xx * 4 + zz) * ROWS, ROWS), ROWS)
@@ -297,6 +343,16 @@
         gather_stage(4, k)
         project(k)
 
+    @pl.when(turned == 1)
+    def _():
+        for which in range(2):
+            code_send(which, device(ox, z, which)).start()
+
+    @pl.when(turned == 0)
+    def _():
+        code_send(other, to_sib).start()
+        code_keep().start()
+
     q_scale = math.log2(math.e) / math.sqrt(HD)
 
     def rotated(cols):
@@ -376,10 +432,8 @@
 
     def finish(block, j, total):
         cols = half_cols(core, j)
-        is_own = core == block
-        own = codes[:, cols]
-        sib = sib_codes[:, j * JC : (j + 1) * JC]
-        resid = jnp.where(is_own, own.astype(F32), sib.astype(F32)) * row_scale(block, cols)
+        coded_in = resid_codes[block, :, j * JC : (j + 1) * JC]
+        resid = coded_in.astype(F32) * tables[0:1, cols]
         codes4 = jnp.clip(total * tables[2:3, cols], -7.0, 7.0).astype(BF)
         updated = resid + codes4.astype(F32) * tables[3:4, cols]
         coded = jnp.clip(updated * tables[4:5, cols], -127.0, 127.0).astype(BF)
@@ -390,11 +444,8 @@
             out.at[:, cols],
             pp_send.at[block, j],
             pp_recv.at[slot],
-            device(x, z, block, 1),
+            device(fx, z, block, 1),
         )
-
-    def row_scale(block, cols):
-        return tables[0:1, cols]
 
     across = ((0, zn, to_next), (1, zp, to_prev), (2, zo, to_far))
 
@@ -407,29 +458,28 @@
                 rows = slice(part * (BLOCK // 2), (part + 1) * (BLOCK // 2))
                 ref[part] = add(ref[part], from_sib[block, j, rows, :]).astype(BF)
             if x_first:
-                hand(block, j, 1, ref.at[ox], from_x.at[block, j], to_x)
+                hand(block, j, 1, ref.at[gx], from_x.at[block, j], to_x)
             else:
                 for slot, zz, peer in across:
                     hand(block, j, 1 + slot, ref.at[:, z_rows(zz), :], from_z.at[block, j, slot], peer)
         elif x_first and stage == 1:
             got(block, j, 1)
-            ref[x] = add(ref[x], from_x[block, j]).astype(BF)
+            ref[fx] = add(ref[fx], from_x[block, j]).astype(BF)
             for slot, zz, peer in across:
-                hand(block, j, 2 + slot, ref.at[x, z_rows(zz), :], from_z.at[block, j, slot, 0], peer)
+                hand(block, j, 2 + slot, ref.at[fx, z_rows(zz), :], from_z.at[block, j, slot, 0], peer)
         elif x_first:
             got(block, j, 2, 3, 4)
             parts = [from_z[block, j, slot, 0] for slot in range(3)]
-            finish(block, j, add(ref[x, z_rows(z), :], *parts))
+            finish(block, j, add(ref[fx, z_rows(z), :], *parts))
         elif stage == 1:
             got(block, j, 1, 2, 3)
             parts = [from_z[block, j, slot] for slot in range(3)]
             ref[:, z_rows(z), :] = add(ref[:, z_rows(z), :], *parts).astype(BF)
-            hand(block, j, 4, ref.at[ox, z_rows(z), :], from_x.at[block, j, 0:ROWS, :], to_x)
+            hand(block, j, 4, ref.at[gx, z_rows(z), :], from_x.at[block, j, 0:ROWS, :], to_x)
         else:
             got(block, j, 4)
-            finish(block, j, add(ref[x, z_rows(z), :], from_x[block, j, 0:ROWS, :]))
-
-    code_copy.wait_recv()
+            finish(block, j, add(ref[fx, z_rows(z), :], from_x[block, j, 0:ROWS, :]))
+
     attend(0, lambda chunk: None)
     loads[3].wait()
 
@@ -441,24 +491,46 @@
             after(j)
         reduce_stage(0, block, NJ - 1)
 
-    def serve(chunk):
-        if chunk >= 4:
-            reduce_stage(1, 0, chunk - 4)
+    def beside_attention(chunk):
+        if chunk >= 6:
+            reduce_stage(1, 0, chunk - 6)
+
+    def beside_output(j):
+        if j < 2:
+            reduce_stage(1, 0, j + 2)
+        else:
+            reduce_stage(2, 0, j - 2)
 
     run_produce(0, lambda j: None)
-    attend(1, serve)
-    run_produce(1, lambda j: reduce_stage(2, 0, j))
+    attend(1, beside_attention)
+    for block in range(2):
+        pltpu.make_async_copy(
+            codes.at[:, half_of(0)], resid_codes.at[block], code_recv_sem.at[block]
+        ).wait()
+    run_produce(1, beside_output)
+    reduce_stage(2, 0, 2)
+    reduce_stage(2, 0, 3)
     for j in range(NJ):
         reduce_stage(1, 1, j)
     for j in range(NJ):
         reduce_stage(2, 1, j)
 
+    for copy in pending:
+        copy.wait_send()
+
+    @pl.when(turned == 1)
+    def _():
+        for which in range(2):
+            code_send(which, device(ox, z, which)).wait_send()
+
+    @pl.when(turned == 0)
+    def _():
+        code_send(other, to_sib).wait_send()
+
     for which in range(2):
         for j in range(NJ):
             ref = out.at[:, pl.ds(which * HALF + j * JC, JC)]
             pltpu.make_async_copy(ref, ref, pp_recv.at[which * NJ + j]).wait()
-    for copy in pending:
-        copy.wait_send()
 
 
 def local(
@@ -476,11 +548,18 @@
 ):
     half = np.power(np.float64(ROPE_BASE), -2.0 * np.arange(HD // 2) / HD).astype(np.float32)
     freqs = jnp.asarray(np.concatenate([half, half])[None, :])
-    vmem = pl.BlockSpec(memory_space=pltpu.VMEM)
-    smem = pl.BlockSpec(memory_space=pltpu.SMEM)
     hbm = pl.BlockSpec(memory_space=pl.ANY)
     dma = pltpu.SemaphoreType.DMA
+    smem = pltpu.SMEM
     scratch = [
+        pltpu.VMEM((ROWS, D), BF),
+        smem((1, D // HD), jnp.int32),
+        smem((1,), jnp.int32),
+        pltpu.VMEM((1, D), BF),
+        pltpu.VMEM((1, HD), F32),
+        smem((1, D // HD), jnp.int32),
+        smem((1, D // HD), jnp.int32),
+        smem((SECTIONS, D // HD), jnp.int32),
         pltpu.VMEM((NK, TOKENS, KC), BF),
         pltpu.VMEM((D, HEADS * HD), BF),
         pltpu.VMEM((D, 2 * HD), BF),
@@ -501,12 +580,14 @@
         pltpu.VMEM((2, NJ, BLOCK // 2, JC), BF),
         pltpu.VMEM((2, NJ, 3, 2, ROWS, JC), BF),
         pltpu.VMEM((2, NJ, ROWS, JC), BF),
-        pltpu.VMEM((ROWS, HALF), BF),
+        pltpu.VMEM((2, ROWS, HALF), BF),
+        dma((8,)),
         dma((4,)),
         dma((NK, 10)),
         dma((NK, 10)),
         dma((2 * NJ, 6)),
         dma((2 * NJ, 6)),
+        dma((2,)),
         dma((2,)),
         dma((2, NJ)),
         dma((2 * NJ,)),
@@ -514,7 +595,7 @@
     received = pl.pallas_call(
         kernel,
         out_shape=jax.ShapeDtypeStruct((ROWS, D), BF),
-        in_specs=[vmem, smem, smem, vmem, vmem, hbm, hbm, hbm, hbm, smem, smem, smem],
+        in_specs=[hbm] * 12,
         out_specs=hbm,
         scratch_shapes=scratch,
         compiler_params=pltpu.CompilerParams(

time: 74.6 us -> 71.5 us (0.958)
  Pallas kernels: 72.1 us -> 69 us
    pallas_call x1, Pallas kernels: 72.1 us -> 69 us  [local(): pl.pallas_call(kernel, out_shape=jax.ShapeDtypeStruct((ROWS, D), BF), in_...]
where the time goes in v3:
time: 71.5 us; the launch traced here: 71.4 us
  Pallas kernels  69 us (97%)
  local copies, waits for them, and re-layouts  1.67 us (2%)
    pallas_call x1, Pallas kernels, local(): pl.pallas_call(kernel, out_shape=jax.ShapeDtypeStruct((ROWS, D), BF), in_...  69 us
    unnamed x1, local copies, waits for them, and re-layouts  1.67 us

profile of v3, /device:TPU:1, one launch (start us, length us, event | category | flops | bytes accessed | tf_op | source)
XLA Modules:
  0.0 71.4 jit_solution(10493342336437844929)
XLA Ops:
  0.7 69.0 %relay_section.1 = bf16[16,8192]{1,0:T(8,128)(2,1)} custom-call(bf16[16,8192]{1,0:T(8,128)(2,1)} %bitcast.11, s32[1,64]{1,0:T(1,128)} %in_exps_hbm.1, s32[1]{0:T(128)S(6)} %copy.14.prefix_hbm, bf16[1,8192]{1,0:T(2,128)(2,1)} %gain_hbm.1, f32[1,128]{1,0:T(1,128)} %constant.2.clone.freqs_hbm, bf16[8192,512]{1,0:T(8,128)(2,1)} %bitcast.7, ...), custom_call_target="tpu_custom_call" | custom-call | flops 10000000000 | bytes 27262976 | tf_op jit(solution)/shard_map/relay_section/pallas_call | solution.py:595
  69.7 1.7 %copy.15 = bf16[1,16,8192]{2,1,0:T(8,128)(2,1)} copy(bf16[1,16,8192]{2,1,0:T(8,128)(2,1)} %bitcast.6) | data formatting | bytes 524288

commit v4 on v3

--- a/solution.py
+++ b/solution.py
@@ -51,7 +51,7 @@
     codes_hbm,
     in_exps_hbm,
     prefix_hbm,
-    gain_hbm,
+    gain,
     freqs_hbm,
     wq_hbm,
     wkv_hbm,
@@ -64,7 +64,6 @@
     codes,
     in_exps,
     prefix_len,
-    gain,
     freqs,
     part_exps,
     share_exps,
@@ -130,7 +129,6 @@
         for i, (src, dst) in enumerate(
             (
                 (codes_hbm, codes),
-                (gain_hbm, gain),
                 (in_exps_hbm, in_exps),
                 (part_exps_hbm, part_exps),
                 (share_exps_hbm, share_exps),
@@ -548,6 +546,7 @@
 ):
     half = np.power(np.float64(ROPE_BASE), -2.0 * np.arange(HD // 2) / HD).astype(np.float32)
     freqs = jnp.asarray(np.concatenate([half, half])[None, :])
+    vmem = pl.BlockSpec(memory_space=pltpu.VMEM)
     hbm = pl.BlockSpec(memory_space=pl.ANY)
     dma = pltpu.SemaphoreType.DMA
     smem = pltpu.SMEM
@@ -555,7 +554,6 @@
         pltpu.VMEM((ROWS, D), BF),
         smem((1, D // HD), jnp.int32),
         smem((1,), jnp.int32),
-        pltpu.VMEM((1, D), BF),
         pltpu.VMEM((1, HD), F32),
         smem((1, D // HD), jnp.int32),
         smem((1, D // HD), jnp.int32),
@@ -581,7 +579,7 @@
         pltpu.VMEM((2, NJ, 3, 2, ROWS, JC), BF),
         pltpu.VMEM((2, NJ, ROWS, JC), BF),
         pltpu.VMEM((2, ROWS, HALF), BF),
-        dma((8,)),
+        dma((7,)),
         dma((4,)),
         dma((NK, 10)),
         dma((NK, 10)),
@@ -595,7 +593,7 @@
     received = pl.pallas_call(
         kernel,
         out_shape=jax.ShapeDtypeStruct((ROWS, D), BF),
-        in_specs=[hbm] * 12,
+        in_specs=[hbm] * 3 + [vmem] + [hbm] * 8,
         out_specs=hbm,
         scratch_shapes=scratch,
         compiler_params=pltpu.CompilerParams(

time: 71.5 us -> 72.3 us (1.011)
  Pallas kernels: 69 us -> 69.8 us
    pallas_call x1, Pallas kernels: 69 us -> 69.8 us  [local(): pl.pallas_call(kernel, out_shape=jax.ShapeDtypeStruct((ROWS, D), BF), in_...]
where the time goes in v4:
time: 72.3 us; the launch traced here: 72.1 us
  Pallas kernels  69.8 us (97%)
  local copies, waits for them, and re-layouts  1.67 us (2%)
    pallas_call x1, Pallas kernels, local(): pl.pallas_call(kernel, out_shape=jax.ShapeDtypeStruct((ROWS, D), BF), in_...  69.8 us
    unnamed x1, local copies, waits for them, and re-layouts  1.67 us

profile of v4, /device:TPU:1, one launch (start us, length us, event | category | flops | bytes accessed | tf_op | source)
XLA Modules:
  0.0 72.1 jit_solution(16859736133049433696)
XLA Ops:
  0.7 69.8 %relay_section.1 = bf16[16,8192]{1,0:T(8,128)(2,1)} custom-call(bf16[16,8192]{1,0:T(8,128)(2,1)} %bitcast.11, s32[1,64]{1,0:T(1,128)} %in_exps_hbm.1, s32[1]{0:T(128)S(6)} %copy.14.prefix_hbm, bf16[1,8192]{1,0:T(2,128)(2,1)} %gain.1, f32[1,128]{1,0:T(1,128)} %constant.2.clone.freqs_hbm, bf16[8192,512]{1,0:T(8,128)(2,1)} %bitcast.7, ...), custom_call_target="tpu_custom_call" | custom-call | flops 10000000000 | bytes 27262976 | tf_op jit(solution)/shard_map/relay_section/pallas_call | solution.py:593
  70.4 1.7 %copy.15 = bf16[1,16,8192]{2,1,0:T(8,128)(2,1)} copy(bf16[1,16,8192]{2,1,0:T(8,128)(2,1)} %bitcast.6) | data formatting | bytes 524288
